TPU v7x, 32 devices: a whole 2x2x4 slice. The times are simulated.
32 devices in a mesh: ep: 4 (over y, x), blk: 8 (over z, core).
Axes of the slice: x: 2, y: 2, z: 4, core: 2. Of those that a mesh axis runs over, the one named last changes fastest.
Arguments:
- tokens: bfloat16 [4096, 7168], P(('ep', 'blk')), may hold values from -6 to 6
- route: int32 [4096, 8], P(('ep', 'blk')), may hold values from 0 to 255, as said below
- gates: float32 [4096, 8], P(('ep', 'blk')), may hold values from 0.1 to 1
- cotangent: bfloat16 [4096, 7168], P(('ep', 'blk')), may hold values from -6 to 6
- w_gate: bfloat16 [4, 7168, 2048], P('ep', None, 'blk'), may hold values from -0.0625 to 0.0625
- w_up: bfloat16 [4, 7168, 2048], P('ep', None, 'blk'), may hold values from -0.0625 to 0.0625
- w_down: bfloat16 [4, 2048, 7168], P('ep', 'blk'), may hold values from -0.125 to 0.125
Outputs:
- mixed: bfloat16 [4096, 7168], P(('ep', 'blk'))
- grad_tokens: bfloat16 [4096, 7168], P(('ep', 'blk'))
- grad_gate: bfloat16 [4, 7168, 2048], P('ep', None, 'blk')
- grad_up: bfloat16 [4, 7168, 2048], P('ep', None, 'blk')
- grad_down: bfloat16 [4, 2048, 7168], P('ep', 'blk')
Inputs may be any that keep to these rules, and one draw needn't show every extreme that they name: `route`: each row names 8 different experts; numbers below 4 are the window's experts. Among the 128 rows of one device each window expert is named by 1 to 4 rows, and in every draw one window expert is named by exactly 4 rows on every device.
All inputs are finite; a program needn't handle non-finite values.
Results may differ from a plain program's by a relative error of at most 0.025.
Values may be sent and summed in bfloat16 or wider, within the bound.
A program may use at most 192 MiB of HBM per device.

v0:
```python
import jax
import jax.numpy as jnp
from jax import lax
from jax.sharding import PartitionSpec as P

CAP = 4


def local(tokens, route, gates, cotangent, w_gate, w_up, w_down):
    groups = lax.axis_size("ep")
    model_width = tokens.shape[1]
    matches = route[:, :, None] == jnp.arange(groups, dtype=jnp.int32)
    member = jnp.any(matches, axis=1)
    weight = jnp.sum(jnp.where(matches, gates[:, :, None], 0.0), axis=1)
    places = jnp.cumsum(member.astype(jnp.int32), axis=0) - 1
    picked = member[:, :, None] & (places[:, :, None] == jnp.arange(CAP, dtype=jnp.int32))
    picked_b = picked.astype(jnp.bfloat16)
    picked_w = jnp.where(picked, weight[:, :, None], 0.0)
    slot_gate = jnp.sum(picked_w, axis=0)
    x_slots = jnp.einsum(
        "tec,td->ecd", picked_b, tokens, preferred_element_type=jnp.float32
    ).astype(jnp.bfloat16)
    d_rows = jnp.einsum("tec,td->ecd", picked_b, cotangent, preferred_element_type=jnp.float32)
    d_slots = (d_rows * slot_gate[:, :, None]).astype(jnp.bfloat16)
    moved_x, moved_d = (
        lax.all_to_all(x_slots, "ep", split_axis=0, concat_axis=0, tiled=True),
        lax.all_to_all(d_slots, "ep", split_axis=0, concat_axis=0, tiled=True),
    )
    rows_x, rows_d = (
        lax.all_gather(moved_x.reshape(-1, model_width), "blk", axis=0, tiled=True),
        lax.all_gather(moved_d.reshape(-1, model_width), "blk", axis=0, tiled=True),
    )
    gate_pre = jnp.dot(rows_x, w_gate[0], preferred_element_type=jnp.float32)
    up_pre = jnp.dot(rows_x, w_up[0], preferred_element_type=jnp.float32)
    logistic = jax.nn.sigmoid(gate_pre)
    hidden = (gate_pre * logistic * up_pre).astype(jnp.bfloat16)
    expert_rows = lax.psum_scatter(
        jnp.dot(hidden, w_down[0], preferred_element_type=jnp.float32).astype(jnp.bfloat16),
        "blk",
        scatter_dimension=0,
        tiled=True,
    ).astype(jnp.float32)
    expert_rows = expert_rows.astype(jnp.bfloat16).reshape(groups, CAP, model_width)
    hidden_grad = jnp.einsum("rd,fd->rf", rows_d, w_down[0], preferred_element_type=jnp.float32)
    grad_down = jnp.einsum("rf,rd->fd", hidden, rows_d, preferred_element_type=jnp.float32).astype(
        jnp.bfloat16
    )
    slope = logistic * (1.0 + gate_pre * (1.0 - logistic))
    gate_grad = (hidden_grad * up_pre * slope).astype(jnp.bfloat16)
    up_grad = (hidden_grad * gate_pre * logistic).astype(jnp.bfloat16)
    grad_gate = jnp.einsum(
        "rd,rf->df", rows_x, gate_grad, preferred_element_type=jnp.float32
    ).astype(jnp.bfloat16)
    grad_up = jnp.einsum("rd,rf->df", rows_x, up_grad, preferred_element_type=jnp.float32).astype(
        jnp.bfloat16
    )
    first = jnp.einsum("rf,df->rd", gate_grad, w_gate[0], preferred_element_type=jnp.float32)
    second = jnp.einsum("rf,df->rd", up_grad, w_up[0], preferred_element_type=jnp.float32)
    input_rows = lax.psum_scatter(
        (first + second).astype(jnp.bfloat16), "blk", scatter_dimension=0, tiled=True
    ).astype(jnp.float32)
    input_rows = input_rows.astype(jnp.bfloat16).reshape(groups, CAP, model_width)
    back_out, back_in = (
        lax.all_to_all(expert_rows, "ep", split_axis=0, concat_axis=0, tiled=True),
        lax.all_to_all(input_rows, "ep", split_axis=0, concat_axis=0, tiled=True),
    )
    mixed = jnp.einsum(
        "tec,ecd->td", picked_w, back_out.astype(jnp.float32), precision=lax.Precision.HIGHEST
    ).astype(jnp.bfloat16)
    grad_tokens = jnp.einsum(
        "tec,ecd->td", picked_b, back_in, preferred_element_type=jnp.float32
    ).astype(jnp.bfloat16)
    return (mixed, grad_tokens, grad_gate[None], grad_up[None], grad_down[None])


def solution(mesh):
    return jax.shard_map(
        local,
        mesh=mesh,
        in_specs=(
            P(("ep", "blk"), None),
            P(("ep", "blk"), None),
            P(("ep", "blk"), None),
            P(("ep", "blk"), None),
            P("ep", None, "blk"),
            P("ep", None, "blk"),
            P("ep", "blk", None),
        ),
        out_specs=(
            P(("ep", "blk"), None),
            P(("ep", "blk"), None),
            P("ep", None, "blk"),
            P("ep", None, "blk"),
            P("ep", "blk", None),
        ),
        check_vma=False,
    )
```

profile of v0, /device:TPU:0, one launch (start us, length us, event | category | flops | bytes accessed | tf_op | source)
XLA Modules:
  0.0 176.3 jit_solution(6211346877765354240)
XLA Ops:
  7.2 0.8 fusion.21
  8.1 0.1 copy.29
  8.2 0.2 reduce_window_sum.11
  8.4 0.7 select_reduce_fusion
  9.3 0.4 convolution_convert_fusion.4
  9.6 10.6 %all_to_all.20 = bf16[4,4,7168]{2,1,0:T(4,128)(2,1)S(1)} all-to-all(bf16[4,4,7168]{2,1,0:T(4,128)(2,1)S(1)} %convolution_convert_fusion.4), channel_id=1, replica_groups=mesh['ep'=4,'blk'=8] {'ep'}, dimensions={0} | all-to-all | bytes 458752 | tf_op jit(solution)/shard_map/all_to_all | solution.py:26
  20.2 0.7 reshape.36
  21.1 1.9 %fusion.6 = bf16[4,4,7168]{2,1,0:T(4,128)(2,1)S(1)} fusion(bf16[128,7168]{1,0:T(8,128)(2,1)} %param.10, f32[4,4]{1,0:T(4,128)S(1)} %copy.34, pred[128,4,4]{0,1,2:T(4,128)(4,1)S(1)} %get-tuple-element.6), kind=kOutput, calls=%fused_computation.14 | convolution fusion | flops 29589504 | bytes 2066496 | tf_op jit(solution)/shard_map/tec,td->ecd/dot_general | solution.py:23
  23.0 8.0 %all_to_all.21 = bf16[4,4,7168]{2,1,0:T(4,128)(2,1)S(1)} all-to-all(bf16[4,4,7168]{2,1,0:T(4,128)(2,1)S(1)} %fusion.6), channel_id=1, replica_groups=mesh['ep'=4,'blk'=8] {'ep'}, dimensions={0} | all-to-all | bytes 458752 | tf_op jit(solution)/shard_map/all_to_all | solution.py:27
  31.0 0.7 reshape.38
  31.8 15.9 %all-gather.3.cloned.1.call-done = bf16[128,7168]{1,0:T(8,128)(2,1)} async-done(((bf16[16,7168]{1,0:T(8,128)(2,1)}), bf16[128,7168]{1,0:T(8,128)(2,1)}) %all-gather.3.cloned.1.call-update) | async-done | bytes 1835024 | tf_op jit(solution)/shard_map/all_gather | solution.py:30
  47.7 3.4 %fusion.11 = f32[128,256]{1,0:T(8,128)S(1)} fusion(bf16[128,7168]{1,0:T(8,128)(2,1)} %all-gather.3.cloned.1.call-done, bf16[1,7168,256]{2,1,0:T(8,128)(2,1)} %param.12), kind=kOutput, calls=%fused_computation.20 | convolution fusion | flops 469762048 | bytes 5636096 | tf_op jit(solution)/shard_map/dot_general | solution.py:34
  51.1 0.8 copy-done.3
  51.9 0.6 fusion.15
  52.6 23.8 %all-gather.5.cloned.1.call-done = bf16[128,7168]{1,0:T(8,128)(2,1)} async-done(((bf16[16,7168]{1,0:T(8,128)(2,1)}), bf16[128,7168]{1,0:T(8,128)(2,1)}) %all-gather.5.cloned.1.call-update) | async-done | bytes 1835024 | tf_op jit(solution)/shard_map/all_gather | solution.py:31
  76.4 4.1 %multiply_convert_fusion = (bf16[128,256]{1,0:T(8,128)(2,1)S(1)}, bf16[128,256]{1,0:T(8,128)(2,1)S(1)}, bf16[128,256]{1,0:T(8,128)(2,1)S(1)}) fusion(f32[128,256]{1,0:T(8,128)S(1)} %fusion.15, f32[128,256]{1,0:T(8,128)S(1)} %fusion.11, bf16[128,7168]{1,0:T(8,128)(2,1)} %all-gather.5.cloned.1.call-done, bf16[1,256,7168]{2,1,0:T(8,128)(2,1)} %param.13), kind=kOutput, calls=%fused_computation.30 | convolution fusion | flops 470286336 | bytes 5963776 | tf_op jit(solution)/shard_map/rd,fd->rf/dot_general | solution.py:44
  80.5 1.3 fusion.13
  81.9 0.7 copy-done.5
  82.6 2.6 %fusion.4 = bf16[128,7168]{1,0:T(8,128)(2,1)} fusion(f32[128,7168]{1,0:T(8,128)S(1)} %fusion.13, bf16[128,256]{1,0:T(8,128)(2,1)S(1)} %get-tuple-element.7, bf16[1,7168,256]{2,1,0:T(8,128)(2,1)S(1)} %copy-done.5), kind=kOutput, calls=%fused_computation.10 | convolution fusion | flops 471597056 | bytes 9240576 | tf_op jit(solution)/shard_map/rf,df->rd/dot_general | solution.py:58
  85.2 3.9 %convolution_convert_fusion.3 = bf16[128,7168]{1,0:T(8,128)(2,1)} fusion(bf16[128,256]{1,0:T(8,128)(2,1)S(1)} %get-tuple-element.9, bf16[1,256,7168]{2,1,0:T(8,128)(2,1)} %param.13), kind=kOutput, calls=%fused_computation.12 | convolution fusion | flops 470679552 | bytes 5570560 | tf_op jit(solution)/shard_map/dot_general | solution.py:38
  89.2 4.6 %fusion = bf16[1,7168,256]{2,1,0:T(8,128)(2,1)} fusion(bf16[128,7168]{1,0:T(8,128)(2,1)} %all-gather.3.cloned.1.call-done, bf16[128,256]{1,0:T(8,128)(2,1)S(1)} %get-tuple-element.8), kind=kOutput, calls=%fused_computation.3 | convolution fusion | flops 471597056 | bytes 5570560 | tf_op jit(solution)/shard_map/rd,rf->df/dot_general | solution.py:51
  93.8 3.0 %fusion.1 = bf16[1,7168,256]{2,1,0:T(8,128)(2,1)} fusion(bf16[128,7168]{1,0:T(8,128)(2,1)S(1)} %copy-done.2, bf16[128,256]{1,0:T(8,128)(2,1)S(1)} %get-tuple-element.7), kind=kOutput, calls=%fused_computation.4 | convolution fusion | flops 471597056 | bytes 5570560 | tf_op jit(solution)/shard_map/rd,rf->df/dot_general | solution.py:54
  96.8 23.2 %reduce-scatter.5.cloned.1.call-done = bf16[16,7168]{1,0:T(8,128)(2,1)} async-done(((bf16[128,7168]{1,0:T(8,128)(2,1)}), bf16[16,7168]{1,0:T(8,128)(2,1)}) %reduce-scatter.5.cloned.1.call-update) | async-done | bytes 229392 | tf_op jit(solution)/shard_map/reduce_scatter | solution.py:59
  120.0 1.7 reshape.39
  121.7 3.7 %all-to-all-start.3 = ((bf16[4,4,7168]{2,1,0:T(4,128)(2,1)}), bf16[4,4,7168]{2,1,0:T(4,128)(2,1)S(1)}, u32[]{:S(2)}, u32[]{:S(2)}) async-start(bf16[4,4,7168]{2,1,0:T(4,128)(2,1)} %reshape.39), calls=%async_computation.5 | async-start | bytes 458752 | tf_op jit(solution)/shard_map/all_to_all | solution.py:65
  125.4 4.5 %fusion.2 = bf16[1,256,7168]{2,1,0:T(8,128)(2,1)} fusion(bf16[128,256]{1,0:T(8,128)(2,1)S(1)} %get-tuple-element.9, bf16[128,7168]{1,0:T(8,128)(2,1)} %all-gather.5.cloned.1.call-done), kind=kOutput, calls=%fused_computation.5 | convolution fusion | flops 471597056 | bytes 5570560 | tf_op jit(solution)/shard_map/rf,rd->fd/dot_general | solution.py:45
  129.9 26.2 %reduce-scatter.3.cloned.1.call-done = bf16[16,7168]{1,0:T(8,128)(2,1)} async-done(((bf16[128,7168]{1,0:T(8,128)(2,1)}), bf16[16,7168]{1,0:T(8,128)(2,1)}) %reduce-scatter.3.cloned.1.call-update) | async-done | bytes 229392 | tf_op jit(solution)/shard_map/reduce_scatter | solution.py:37
  156.1 1.7 reshape.37
  157.8 3.8 %all-to-all-start.1 = ((bf16[4,4,7168]{2,1,0:T(4,128)(2,1)}), bf16[4,4,7168]{2,1,0:T(4,128)(2,1)S(1)}, u32[]{:S(2)}, u32[]{:S(2)}) async-start(bf16[4,4,7168]{2,1,0:T(4,128)(2,1)} %reshape.37), calls=%async_computation.2 | async-start | bytes 458752 | tf_op jit(solution)/shard_map/all_to_all | solution.py:64
  161.6 2.0 %fusion.5 = bf16[128,7168]{1,0:T(8,128)(2,1)} fusion(pred[128,4,4]{0,1,2:T(4,128)(4,1)S(1)} %get-tuple-element.6, bf16[4,4,7168]{2,1,0:T(4,128)(2,1)S(1)} %all-to-all-done.3), kind=kOutput, calls=%fused_computation.11 | convolution fusion | flops 30277632 | bytes 2066432 | tf_op jit(solution)/shard_map/tec,ecd->td/dot_general | solution.py:70
  163.6 3.3 %all-to-all-done.1 = bf16[4,4,7168]{2,1,0:T(4,128)(2,1)S(1)} async-done(((bf16[4,4,7168]{2,1,0:T(4,128)(2,1)}), bf16[4,4,7168]{2,1,0:T(4,128)(2,1)S(1)}, u32[]{:S(2)}, u32[]{:S(2)}) %all-to-all-start.1) | async-done | bytes 229408 | tf_op jit(solution)/shard_map/all_to_all | solution.py:64
  166.9 2.9 %fusion.3 = bf16[128,7168]{1,0:T(8,128)(2,1)} fusion(bf16[4,4,7168]{2,1,0:T(4,128)(2,1)S(1)} %all-to-all-done.1, pred[128,4,4]{0,1,2:T(4,128)(4,1)S(1)} %get-tuple-element.6, f32[128,4]{0,1:T(4,128)S(1)} %select_reduce_fusion), kind=kOutput, calls=%fused_computation.9 | convolution fusion | flops 177080320 | bytes 2068480 | tf_op jit(solution)/shard_map/tec,ecd->td/dot_general | solution.py:67
  (24 shorter events, 0.5 us)
Async XLA Ops:
  7.2 2.1 %copy-start = (bf16[128,7168]{1,0:T(8,128)(2,1)S(1)}, bf16[128,7168]{1,0:T(8,128)(2,1)}, u32[]{:S(2)}) copy-start(bf16[128,7168]{1,0:T(8,128)(2,1)} %param.7) | copy-start | bytes 5505028
  7.2 40.5 %all-gather.3.cloned.1.call-start = ((), (), s32[]{:S(2)}) async-start(), calls=%async_computation.6 | async-start | bytes 2064384 | tf_op jit(solution)/shard_map/all_gather | solution.py:30
  21.0 55.4 %all-gather.5.cloned.1.call-start = ((), (), s32[]{:S(2)}) async-start(), calls=%async_computation.8 | async-start | bytes 2064384 | tf_op jit(solution)/shard_map/all_gather | solution.py:31
  31.8 88.2 %reduce-scatter.5.cloned.1.call-start = ((), (), s32[]{:S(2)}) async-start(), calls=%async_computation.9 | async-start | bytes 2064384 | tf_op jit(solution)/shard_map/reduce_scatter | solution.py:59
  47.7 3.4 %copy-start.1 = (bf16[128,7168]{1,0:T(8,128)(2,1)S(1)}, bf16[128,7168]{1,0:T(8,128)(2,1)}, u32[]{:S(2)}) copy-start(bf16[128,7168]{1,0:T(8,128)(2,1)} %all-gather.3.cloned.1.call-done) | copy-start | bytes 5505028
  47.7 4.2 %copy-start.3 = (bf16[1,7168,256]{2,1,0:T(8,128)(2,1)S(1)}, bf16[1,7168,256]{2,1,0:T(8,128)(2,1)}, u32[]{:S(2)}) copy-start(bf16[1,7168,256]{2,1,0:T(8,128)(2,1)} %param.11) | copy-start | bytes 11010052
  76.4 4.1 %copy-start.4 = (bf16[1,7168,256]{2,1,0:T(8,128)(2,1)S(1)}, bf16[1,7168,256]{2,1,0:T(8,128)(2,1)}, u32[]{:S(2)}) copy-start(bf16[1,7168,256]{2,1,0:T(8,128)(2,1)} %param.11) | copy-start | bytes 11010052
  80.5 2.0 %copy-start.5 = (bf16[1,7168,256]{2,1,0:T(8,128)(2,1)S(1)}, bf16[1,7168,256]{2,1,0:T(8,128)(2,1)}, u32[]{:S(2)}) copy-start(bf16[1,7168,256]{2,1,0:T(8,128)(2,1)} %param.12) | copy-start | bytes 11010052
  85.1 70.9 %reduce-scatter.3.cloned.1.call-start = ((), (), s32[]{:S(2)}) async-start(), calls=%async_computation.7 | async-start | bytes 2064384 | tf_op jit(solution)/shard_map/reduce_scatter | solution.py:37
  89.1 4.6 %copy-start.2 = (bf16[128,7168]{1,0:T(8,128)(2,1)S(1)}, bf16[128,7168]{1,0:T(8,128)(2,1)}, u32[]{:S(2)}) copy-start(bf16[128,7168]{1,0:T(8,128)(2,1)} %all-gather.3.cloned.1.call-done) | copy-start | bytes 5505028
  121.7 36.1 %all-to-all-start.3 = ((bf16[4,4,7168]{2,1,0:T(4,128)(2,1)}), bf16[4,4,7168]{2,1,0:T(4,128)(2,1)S(1)}, u32[]{:S(2)}, u32[]{:S(2)}) async-start(bf16[4,4,7168]{2,1,0:T(4,128)(2,1)} %reshape.39), calls=%async_computation.5 | async-start | bytes 458752 | tf_op jit(solution)/shard_map/all_to_all | solution.py:65
  157.8 9.1 %all-to-all-start.1 = ((bf16[4,4,7168]{2,1,0:T(4,128)(2,1)}), bf16[4,4,7168]{2,1,0:T(4,128)(2,1)S(1)}, u32[]{:S(2)}, u32[]{:S(2)}) async-start(bf16[4,4,7168]{2,1,0:T(4,128)(2,1)} %reshape.37), calls=%async_computation.2 | async-start | bytes 458752 | tf_op jit(solution)/shard_map/all_to_all | solution.py:64
Sparse Core Ops, SparseCore 0:
  21.1 26.5 all-gather.2
  49.9 26.4 all-gather.4
  85.3 34.6 reduce-scatter.4
  122.7 33.2 reduce-scatter.2
where the time goes:
time: 177 us; the launch traced here: 176 us
  waiting for transfers between devices  92.5 us (52%)
  matrix products  35.2 us (20%)
  blocking collectives  18.6 us (11%)
  between operations  13.8 us (8%)
  starting transfers between devices  7.64 us (4%)
  local copies, waits for them, and re-layouts  6.74 us (4%)
  other arithmetic  1.85 us (1%)
    reduce_scatter x1, waiting for transfers between devices, local(): lax.psum_scatter(jnp.dot(hidden, w_down[0], preferred_element_type=jnp.fl...  26.2 us
    all_gather x1, waiting for transfers between devices, local(): lax.all_gather(moved_d.reshape(-1, model_width), 'blk', axis=0, tiled=True)  23.8 us
    reduce_scatter x1, waiting for transfers between devices, local(): lax.psum_scatter((first + second).astype(jnp.bfloat16), 'blk', scatter_di...  23.2 us
    all_gather x1, waiting for transfers between devices, local(): lax.all_gather(moved_x.reshape(-1, model_width), 'blk', axis=0, tiled=True)  15.9 us
    all_to_all x1, blocking collectives, local(): lax.all_to_all(x_slots, 'ep', split_axis=0, concat_axis=0, tiled=True)  10.6 us
    all_to_all x1, blocking collectives, local(): lax.all_to_all(d_slots, 'ep', split_axis=0, concat_axis=0, tiled=True)  8.01 us
    dot_general x1, matrix products, local(): jnp.einsum('rd,rf->df', rows_x, gate_grad, preferred_element_type=jnp.flo...  4.64 us
    dot_general x1, matrix products, local(): jnp.einsum('rf,rd->fd', hidden, rows_d, preferred_element_type=jnp.float32)  4.48 us
  transfers between devices with their start and end apart: 6, of which 5 were waited for; matrix products, arithmetic and copies ran while one was open for 16% of the time, Pallas kernels for 0%

commit v1 on v0

v1 whole, which is shorter than its diff:
```python
import functools

import jax
import jax.numpy as jnp
from jax import lax
from jax.experimental import pallas as pl
from jax.experimental.pallas import tpu as pltpu
from jax.sharding import PartitionSpec as P

CAP = 4
CUTS = 4
ROWS = CAP * CUTS
TILE = 256
F32 = jnp.float32
BF16 = jnp.bfloat16
MESH = pl.DeviceIdType.MESH


def mm(a, b):
    return jnp.dot(a, b, preferred_element_type=F32)


def mm_nt(a, b):
    return lax.dot_general(a, b, (((1,), (1,)), ((), ())), preferred_element_type=F32)


def place(shape, row_dim, q):
    row = lax.broadcasted_iota(jnp.int32, shape, row_dim)
    col = lax.broadcasted_iota(jnp.int32, shape, 1 - row_dim)
    hit = (row // CAP) * ROWS + q * CAP + row % CAP == col
    return jnp.where(hit, 1.0, 0.0).astype(BF16)


def exchange(
    E, L, pq_ref, sg_ref, tok_hbm, cot_hbm, wg_hbm, wu_hbm, wd_hbm,
    bo_hbm, bi_hbm, xo_hbm, do_hbm, h_ref, a_ref, b_ref,
    tok, cot, wg, wu, wd, xs, ds, xin, din, xg, dg, gp, up,
    yp, ysib, yline, yret, bo, qp, qsib, qline, qret, bi,
    load_sem, out_sem, disp_s, disp_r, gat_s, gat_r, sib_s, sib_r, line_s, line_r, ret_s, ret_r,
):
    ep = lax.axis_index("ep")
    blk = lax.axis_index("blk")
    l = blk // 2
    c = blk % 2
    D = tok.shape[1]
    W = D // CUTS
    R = E * CAP
    rows = 2 * L * R
    sibling = {"blk": 2 * l + (1 - c)}
    right = {"blk": blk + 2}
    left = {"blk": blk - 2}
    has_right = l < L - 1
    has_left = l > 0

    loads = [
        pltpu.make_async_copy(s, d, load_sem.at[i])
        for i, (s, d) in enumerate(
            [(tok_hbm, tok), (cot_hbm, cot), (wg_hbm.at[0], wg), (wu_hbm.at[0], wu), (wd_hbm.at[0], wd)]
        )
    ]
    for cp in loads:
        cp.start()

    barrier = pltpu.get_barrier_semaphore()
    for k in range(1, E):
        pl.semaphore_signal(barrier, inc=1, device_id={"ep": lax.rem(ep + k, E)}, device_id_type=MESH)
    pl.semaphore_signal(barrier, inc=1, device_id=sibling, device_id_type=MESH)

    @pl.when(has_right)
    def _():
        pl.semaphore_signal(barrier, inc=1, device_id=right, device_id_type=MESH)

    @pl.when(has_left)
    def _():
        pl.semaphore_signal(barrier, inc=1, device_id=left, device_id_type=MESH)

    ends = jnp.where(l > 0, 1, 0) + jnp.where(l < L - 1, 1, 0)
    pl.semaphore_wait(barrier, E + ends)

    def remote(src, dst, ss, rs, dev):
        return pltpu.make_async_remote_copy(
            src_ref=src, dst_ref=dst, send_sem=ss, recv_sem=rs, device_id=dev, device_id_type=MESH
        )

    tails = []

    def tail(cond, make):
        tails.append((cond, make))

    def ep_copy(n, src, dst, ss, rs, j):
        return remote(src.at[j], dst.at[ep], ss.at[n, j], rs.at[n, ep], {"ep": j})

    def ep_send(n, src, dst, ss, rs):
        for k in range(1, E):
            j = lax.rem(ep + k, E)
            ep_copy(n, src, dst, ss, rs, j).start()
            tail(None, functools.partial(ep_copy, n, src, dst, ss, rs, j))

    def ep_wait(n, src, dst, ss, rs):
        for k in range(1, E):
            j = lax.rem(ep + k, E)
            remote(src.at[j], dst.at[j], ss.at[n, j], rs.at[n, j], {"ep": j}).wait_recv()

    def select(src, dst, own, scale):
        def step(t, carry):
            at = pl.ds(pl.multiple_of(t * TILE, TILE), TILE)
            acc = jnp.zeros((E * ROWS, TILE), F32)
            for q in range(CUTS):
                acc += mm(pq_ref[q], src[:, pl.ds(pl.multiple_of(q * W + t * TILE, TILE), TILE)])
            if scale:
                acc = acc * sg_ref[...]
            dst[:, :, at] = acc.astype(BF16).reshape(E, ROWS, TILE)
            return carry

        lax.fori_loop(0, W // TILE, step, 0)
        own[ep] = dst[ep]

    def settle(src, dst):
        def step(t, carry):
            at = pl.ds(pl.multiple_of(t * TILE, TILE), TILE)
            part = src[:, :, at].reshape(E * ROWS, TILE)
            for q in range(CUTS):
                out = mm(place((R, E * ROWS), 0, q), part)
                dst[blk, :, pl.ds(pl.multiple_of(q * W + t * TILE, TILE), TILE)] = out.astype(BF16)
            return carry

        lax.fori_loop(0, W // TILE, step, 0)

    def g_copy(n, buf, j, way, dev):
        b = 2 * j + c
        return remote(buf.at[b], buf.at[b], gat_s.at[n, way, j], gat_r.at[n, b], dev)

    def g_got(n, buf, b):
        remote(buf.at[b], buf.at[b], gat_s.at[n, 0, 0], gat_r.at[n, b], sibling).wait_recv()

    def guarded(cond, fn):
        if cond is None:
            fn()
        else:
            pl.when(cond)(fn)

    def g_send(n, buf, s):
        steps = []
        if s < L - 1:
            steps += [(has_right & (l - s >= 0), l - s, 0, right), (has_left & (l + s < L), l + s, 1, left)]
        if s == 0:
            steps += [(None, l, 2, sibling)]
        else:
            steps += [(l - s >= 0, l - s, 2, sibling), (l + s < L, l + s, 2, sibling)]
        for cond, j, way, dev in steps:
            guarded(cond, lambda j=j, way=way, dev=dev: g_copy(n, buf, j, way, dev).start())
            tail(cond, functools.partial(g_copy, n, buf, j, way, dev))

    def g_wait(n, buf, s):
        pl.when(l - 1 - s >= 0)(lambda: g_got(n, buf, 2 * (l - 1 - s) + c))
        pl.when(l + 1 + s < L)(lambda: g_got(n, buf, 2 * (l + 1 + s) + c))

    def g_sib(n, buf):
        for j in range(L):
            g_got(n, buf, 2 * j + (1 - c))

    def s_copy(n, part, sib, j):
        return remote(part.at[2 * j + 1 - c], sib.at[j], sib_s.at[n, j], sib_r.at[n, j], sibling)

    def s_send(n, part, sib):
        for j in range(L):
            s_copy(n, part, sib, j).start()
            tail(None, functools.partial(s_copy, n, part, sib, j))

    def s_wait(n, part, sib):
        for j in range(L):
            s_copy(n, part, sib, j).wait_recv()

    def r_copy(n, part, line, j, up_way, dev):
        k = j + up_way
        return remote(part.at[2 * j + c], line.at[k], line_s.at[n, j], line_r.at[n, k], dev)

    def total(part, sib, lines, b, j):
        def step(t, carry):
            at = pl.ds(pl.multiple_of(t * 1024, 1024), 1024)
            acc = part[b, :, at].astype(F32) + sib[j, :, at].astype(F32)
            for line, k in lines:
                acc += line[k, :, at].astype(F32)
            part[b, :, at] = acc.astype(BF16)
            return carry

        lax.fori_loop(0, D // 1024, step, 0)

    def r_step(n, part, sib, line, s):
        jl = s - (L - 1 - l)
        jr = L - 1 - s + l

        def go(j, up_way, dev, first):
            def fn():
                if not first:
                    k = j + up_way
                    r_copy(n, part, line, j, up_way, dev).wait_recv()
                    total(part, sib, [(line, k)], 2 * j + c, j)
                else:
                    total(part, sib, [], 2 * j + c, j)
                r_copy(n, part, line, j, up_way, dev).start()

            return fn

        lw = has_left & (jl >= 0)
        rw = has_right & (jr < L)
        pl.when(lw & (l == L - 1))(go(jl, 0, left, True))
        pl.when(rw & (l == 0))(go(jr, 1, right, True))
        if L > 2:
            pl.when(lw & (l < L - 1))(go(jl, 0, left, False))
            pl.when(rw & (l > 0))(go(jr, 1, right, False))
        tail(lw, functools.partial(r_copy, n, part, line, jl, 0, left))
        tail(rw, functools.partial(r_copy, n, part, line, jr, 1, right))

    def r_last(n, part, sib, line, ret, back):
        def join(line_slots):
            def fn():
                for k in line_slots:
                    remote(part.at[blk], line.at[k], line_s.at[n, 0], line_r.at[n, k], sibling).wait_recv()
                total(part, sib, [(line, k) for k in line_slots], blk, l)

            return fn

        pl.when(l == 0)(join([l]))
        pl.when(l == L - 1)(join([l + 1]))
        if L > 2:
            pl.when((l > 0) & (l < L - 1))(join([l, l + 1]))

        def step(t, carry):
            at = pl.ds(pl.multiple_of(t * TILE, TILE), TILE)
            acc = jnp.zeros((E * ROWS, TILE), F32)
            for q in range(CUTS):
                own = part[blk, :, pl.ds(pl.multiple_of(q * W + t * TILE, TILE), TILE)]
                acc += mm(place((E * ROWS, R), 1, q), own)
            ret[:, :, at] = acc.astype(BF16).reshape(E, ROWS, TILE)
            return carry

        lax.fori_loop(0, W // TILE, step, 0)
        back[ep] = ret[ep]
        ep_send(n, ret, back, ret_s, ret_r)

    loads[0].wait()
    select(tok, xs, xin, False)
    ep_send(0, xs, xin, disp_s, disp_r)
    loads[1].wait()
    select(cot, ds, din, True)
    ep_send(1, ds, din, disp_s, disp_r)
    ep_wait(0, xs, xin, disp_s, disp_r)
    settle(xin, xg)
    g_send(0, xg, 0)
    ep_wait(1, ds, din, disp_s, disp_r)
    settle(din, dg)
    for s in range(1, L):
        g_wait(0, xg, s - 1)
        g_send(0, xg, s)
    g_send(1, dg, 0)
    g_sib(0, xg)
    x_out = pltpu.make_async_copy(xg, xo_hbm, out_sem.at[0])
    x_out.start()
    loads[2].wait()
    loads[3].wait()

    def both(t, carry):
        at = pl.ds(pl.multiple_of(t * W, TILE), W)
        x = xg[:, :, at].reshape(rows, W)
        gp[...] += mm(x, wg[at, :])
        up[...] += mm(x, wu[at, :])
        return carry

    gp[...] = jnp.zeros_like(gp)
    up[...] = jnp.zeros_like(up)
    lax.fori_loop(0, CUTS, both, 0)
    h_ref[...] = (gp[...] * jax.nn.sigmoid(gp[...]) * up[...]).astype(BF16)
    if L > 1:
        g_wait(1, dg, 0)
        g_send(1, dg, 1)
    loads[4].wait()

    def down(t, carry):
        at = pl.ds(pl.multiple_of(t * 512, 512), 512)
        yp[:, :, at] = mm(h_ref[...], wd[:, at]).astype(BF16).reshape(2 * L, R, 512)
        return carry

    lax.fori_loop(0, D // 512, down, 0)
    s_send(0, yp, ysib)
    if L > 2:
        g_wait(1, dg, 1)
        g_send(1, dg, 2)
    s_wait(0, yp, ysib)
    r_step(0, yp, ysib, yline, 0)
    for s in range(3, L):
        g_wait(1, dg, s - 1)
        g_send(1, dg, s)
        r_step(0, yp, ysib, yline, s - 2)
    g_sib(1, dg)
    d_out = pltpu.make_async_copy(dg, do_hbm, out_sem.at[1])
    d_out.start()

    hg = jnp.zeros((rows, gp.shape[1]), F32)

    def pull(t, carry):
        at = pl.ds(pl.multiple_of(t * W, TILE), W)
        return carry + mm_nt(dg[:, :, at].reshape(rows, W), wd[:, at])

    hg = lax.fori_loop(0, CUTS, pull, hg)
    g = gp[...]
    u = up[...]
    sig = jax.nn.sigmoid(g)
    a_ref[...] = (hg * u * (sig * (1.0 + g * (1.0 - sig)))).astype(BF16)
    b_ref[...] = (hg * g * sig).astype(BF16)
    done = max(1, L - 2)
    if done < L - 1:
        r_step(0, yp, ysib, yline, done)

    def back_rows(t, carry):
        at = pl.ds(pl.multiple_of(t * 512, 512), 512)
        q = mm_nt(a_ref[...], wg[at, :]) + mm_nt(b_ref[...], wu[at, :])
        qp[:, :, at] = q.astype(BF16).reshape(2 * L, R, 512)
        return carry

    lax.fori_loop(0, D // 512, back_rows, 0)
    s_send(1, qp, qsib)
    s_wait(1, qp, qsib)
    r_step(1, qp, qsib, qline, 0)
    r_last(0, yp, ysib, yline, yret, bo)
    for s in range(1, L - 1):
        r_step(1, qp, qsib, qline, s)
    ep_wait(0, yret, bo, ret_s, ret_r)
    o_out = pltpu.make_async_copy(bo, bo_hbm, out_sem.at[2])
    o_out.start()
    r_last(1, qp, qsib, qline, qret, bi)
    ep_wait(1, qret, bi, ret_s, ret_r)
    i_out = pltpu.make_async_copy(bi, bi_hbm, out_sem.at[3])
    i_out.start()
    for cond, make in tails:
        guarded(cond, lambda make=make: make().wait_send())
    for cp in (x_out, d_out, o_out, i_out):
        cp.wait()


def combine(pw_ref, pt_ref, bo_ref, bi_ref, mixed_ref, grad_ref):
    e_rows = bo_ref.shape[0] * ROWS
    width = bo_ref.shape[2]
    y = bo_ref[...].reshape(e_rows, width)
    mixed_ref[...] = (mm(pw_ref[0, 0], y) + mm(pw_ref[1, 0], y)).astype(BF16)
    grad_ref[...] = mm(pt_ref[0], bi_ref[...].reshape(e_rows, width)).astype(BF16)


def local(tokens, route, gates, cotangent, w_gate, w_up, w_down):
    E = lax.axis_size("ep")
    L = lax.axis_size("blk") // 2
    T, D = tokens.shape
    W = D // CUTS
    R = E * CAP
    rows = 2 * L * R
    F = w_gate.shape[2]
    matches = route[:, :, None] == jnp.arange(E, dtype=jnp.int32)
    member = jnp.any(matches, axis=1)
    weight = jnp.sum(jnp.where(matches, gates[:, :, None], 0.0), axis=1)
    earlier = jnp.tril(jnp.ones((T, T), BF16), -1)
    places = mm(earlier, member.astype(BF16)).astype(jnp.int32)
    picked = member[:, :, None] & (places[:, :, None] == jnp.arange(CAP, dtype=jnp.int32))
    picked_w = jnp.where(picked, weight[:, :, None], 0.0)
    slot_gate = jnp.sum(picked_w, axis=0)
    sg = jnp.broadcast_to(slot_gate[:, None, :], (E, CUTS, CAP)).reshape(E * ROWS, 1)
    quarter = jnp.eye(CUTS, dtype=bool)[:, None, None, :, None]

    def spread(m):
        wide = jnp.where(quarter, m[None, :, :, None, :], jnp.zeros((), m.dtype))
        return wide.reshape(CUTS, T, E * ROWS)

    pt = spread(picked.astype(BF16))
    pq = pt.transpose(0, 2, 1)
    hi = picked_w.astype(BF16)
    lo = (picked_w - hi.astype(F32)).astype(BF16)
    pw = jnp.stack([spread(hi), spread(lo)])

    vm = pl.BlockSpec(memory_space=pltpu.VMEM)
    hbm = pl.BlockSpec(memory_space=pl.ANY)
    sds = jax.ShapeDtypeStruct
    msg = pltpu.VMEM((E, ROWS, W), BF16)
    allrows = pltpu.VMEM((2 * L, R, D), BF16)
    own = pltpu.VMEM((L, R, D), BF16)
    line = pltpu.VMEM((L + 1, R, D), BF16)
    dma = pltpu.SemaphoreType.DMA
    bo, bi, rows_x, rows_d, hidden, gate_grad, up_grad = pl.pallas_call(
        functools.partial(exchange, E, L),
        out_shape=(
            sds((E, ROWS, W), BF16),
            sds((E, ROWS, W), BF16),
            sds((2 * L, R, D), BF16),
            sds((2 * L, R, D), BF16),
            sds((rows, F), BF16),
            sds((rows, F), BF16),
            sds((rows, F), BF16),
        ),
        in_specs=[vm, vm, hbm, hbm, hbm, hbm, hbm],
        out_specs=(hbm, hbm, hbm, hbm, vm, vm, vm),
        scratch_shapes=[
            pltpu.VMEM((T, D), BF16),
            pltpu.VMEM((T, D), BF16),
            pltpu.VMEM((D, F), BF16),
            pltpu.VMEM((D, F), BF16),
            pltpu.VMEM((F, D), BF16),
            msg, msg, msg, msg,
            allrows, allrows,
            pltpu.VMEM((rows, F), F32),
            pltpu.VMEM((rows, F), F32),
            allrows, own, line, msg, msg,
            allrows, own, line, msg, msg,
            dma((5,)),
            dma((4,)),
            dma((2, E)),
            dma((2, E)),
            dma((2, 3, L)),
            dma((2, 2 * L)),
            dma((2, L)),
            dma((2, L)),
            dma((2, L)),
            dma((2, L + 1)),
            dma((2, E)),
            dma((2, E)),
        ],
        compiler_params=pltpu.CompilerParams(
            collective_id=0, has_side_effects=True, vmem_limit_bytes=60 * 1024 * 1024
        ),
    )(pq, sg, tokens, cotangent, w_gate, w_up, w_down)

    mixed, grad_tokens = pl.pallas_call(
        combine,
        grid=(CUTS,),
        out_shape=(sds((T, D), BF16), sds((T, D), BF16)),
        in_specs=[
            pl.BlockSpec((2, 1, T, E * ROWS), lambda q: (0, q, 0, 0)),
            pl.BlockSpec((1, T, E * ROWS), lambda q: (q, 0, 0)),
            pl.BlockSpec((E, ROWS, W), lambda q: (0, 0, 0)),
            pl.BlockSpec((E, ROWS, W), lambda q: (0, 0, 0)),
        ],
        out_specs=(pl.BlockSpec((T, W), lambda q: (0, q)), pl.BlockSpec((T, W), lambda q: (0, q))),
    )(pw, pt, bo, bi)

    rows_x = rows_x.reshape(rows, D)
    rows_d = rows_d.reshape(rows, D)
    grad_down = jnp.einsum("rf,rd->fd", hidden, rows_d, preferred_element_type=F32).astype(BF16)
    grad_gate = jnp.einsum("rd,rf->df", rows_x, gate_grad, preferred_element_type=F32).astype(BF16)
    grad_up = jnp.einsum("rd,rf->df", rows_x, up_grad, preferred_element_type=F32).astype(BF16)
    return (mixed, grad_tokens, grad_gate[None], grad_up[None], grad_down[None])


def solution(mesh):
    return jax.shard_map(
        local,
        mesh=mesh,
        in_specs=(
            P(("ep", "blk"), None),
            P(("ep", "blk"), None),
            P(("ep", "blk"), None),
            P(("ep", "blk"), None),
            P("ep", None, "blk"),
            P("ep", None, "blk"),
            P("ep", "blk", None),
        ),
        out_specs=(
            P(("ep", "blk"), None),
            P(("ep", "blk"), None),
            P("ep", None, "blk"),
            P("ep", None, "blk"),
            P("ep", "blk", None),
        ),
        check_vma=False,
    )
```

time: 177 us -> 108 us (0.61)
  waiting for transfers between devices: 92.5 us -> 0 us
  Pallas kernels: 0 us -> 91.2 us
  matrix products: 35.2 us -> 10.8 us
  blocking collectives: 18.6 us -> 0 us
  between operations: 13.8 us -> 0.73 us
  starting transfers between devices: 7.64 us -> 0 us
  local copies, waits for them, and re-layouts: 6.74 us -> 1.26 us
  other arithmetic: 1.85 us -> 3.77 us
    pallas_call x0 -> x2, Pallas kernels: none -> 91.2 us  [the longest x1 86.7 us: local(): pl.pallas_call(functools.partial(exchange, E, L), out_shape=(sds((E, ROWS...]
    reduce_scatter x2 -> x0, waiting for transfers between devices: 49.4 us -> none  [the longest x1 26.2 us: local(): lax.psum_scatter(jnp.dot(hidden, w_down[0], preferred_element_type=jnp.fl...]
    all_gather x2 -> x0, waiting for transfers between devices: 39.7 us -> none  [the longest x1 23.8 us: local(): lax.all_gather(moved_d.reshape(-1, model_width), 'blk', axis=0, tiled=True)]
    dot_general x13 -> x4, matrix products: 35.2 us -> 10.8 us  [the longest x1 4.62 us: local(): jnp.einsum('rd,rf->df', rows_x, up_grad, preferred_element_type=F32)]
    all_to_all x2 -> x0, blocking collectives: 18.6 us -> none  [the longest x1 10.6 us: local(): lax.all_to_all(x_slots, 'ep', split_axis=0, concat_axis=0, tiled=True)]
    all_to_all x2 -> x0, starting transfers between devices: 7.47 us -> none  [the longest x1 3.79 us: local(): lax.all_to_all(expert_rows, 'ep', split_axis=0, concat_axis=0, tiled=True)]
    reshape x4 -> x1, local copies, waits for them, and re-layouts: 4.92 us -> 0.7 us  [local(): jnp.broadcast_to(slot_gate[:, None, :], (E, CUTS, CAP)).reshape(E * ROWS, 1)]
    all_to_all x2 -> x0, waiting for transfers between devices: 3.31 us -> none  [the longest x1 3.31 us: local(): lax.all_to_all(expert_rows, 'ep', split_axis=0, concat_axis=0, tiled=True)]
  transfers between devices with their start and end apart: 6 -> 0, of which waited for: 5 -> 0; matrix products, arithmetic and copies ran while one was open for 16% -> 0% of each run, Pallas kernels for 0% -> 0%
where the time goes in v1:
time: 108 us
  Pallas kernels  91.2 us (84%)
  matrix products  10.8 us (10%)
  other arithmetic  3.77 us (3%)
  local copies, waits for them, and re-layouts  1.26 us (1%)
    pallas_call x1, Pallas kernels, local(): pl.pallas_call(functools.partial(exchange, E, L), out_shape=(sds((E, ROWS...  86.7 us
    dot_general x1, matrix products, local(): jnp.einsum('rd,rf->df', rows_x, up_grad, preferred_element_type=F32)  4.62 us
    pallas_call x1, Pallas kernels, local(): pl.pallas_call(combine, grid=(CUTS,), out_shape=(sds((T, D), BF16), sds((...  4.57 us
    dot_general x1, matrix products, local(): jnp.einsum('rd,rf->df', rows_x, gate_grad, preferred_element_type=F32)  2.98 us
    dot_general x1, matrix products, local(): jnp.einsum('rf,rd->fd', hidden, rows_d, preferred_element_type=F32)  2.98 us

profile of v1, /device:TPU:0, one launch (start us, length us, event | category | flops | bytes accessed | tf_op | source)
XLA Modules:
  0.0 107.8 jit_solution(8650130225336704745)
XLA Ops:
  0.6 0.7 fusion.8
  1.3 0.2 convolution_convert_fusion.3
  1.6 0.1 broadcast_in_dim.137
  1.7 0.1 broadcast_in_dim.138
  1.8 0.7 broadcast_select_fusion.3.pq_ref
  2.5 0.7 select_reduce_fusion
  3.2 0.1 select_reduce_fusion.1
  3.3 0.7 reshape.60.sg_ref
  4.0 86.7 %shard_map.110 = (bf16[4,16,1792]{2,1,0:T(8,128)(2,1)}, bf16[4,16,1792]{2,1,0:T(8,128)(2,1)}, bf16[8,16,7168]{2,1,0:T(8,128)(2,1)}, bf16[8,16,7168]{2,1,0:T(8,12...) custom-call(bf16[4,64,128]{2,1,0:T(8,128)(2,1)} %broadcast_select_fusion.3.pq_ref, ...), custom_call_target="tpu_custom_call" | custom-call | tf_op jit(solution)/shard_map/pallas_call | solution.py:386
  90.7 0.0 copy-start.1
  90.7 0.0 copy-start.2
  90.7 4.6 %fusion.1 = bf16[1,7168,256]{2,1,0:T(8,128)(2,1)} fusion(bf16[128,7168]{1,0:T(8,128)(2,1)} %bitcast.20, bf16[128,256]{1,0:T(8,128)(2,1)} %get-tuple-element.20), kind=kOutput, calls=%fused_computation.4 | convolution fusion | flops 471597056 | bytes 5570560 | tf_op jit(solution)/shard_map/rd,rf->df/dot_general | solution.py:446
  95.4 0.0 copy-done.1
  95.4 0.0 copy-done.2
  95.4 0.0 copy-start
  95.4 0.0 copy-start.3
  95.4 3.0 %fusion.2 = bf16[1,256,7168]{2,1,0:T(8,128)(2,1)} fusion(bf16[128,256]{1,0:T(8,128)(2,1)S(1)} %copy-done.2, bf16[128,7168]{1,0:T(8,128)(2,1)S(1)} %bitcast.22), kind=kOutput, calls=%fused_computation.5 | convolution fusion | flops 471597056 | bytes 5570560 | tf_op jit(solution)/shard_map/rf,rd->fd/dot_general | solution.py:444
  98.3 0.0 copy-done
  98.4 0.0 copy-done.3
  98.4 3.0 %fusion = bf16[1,7168,256]{2,1,0:T(8,128)(2,1)} fusion(bf16[128,7168]{1,0:T(8,128)(2,1)S(1)} %bitcast.21, bf16[128,256]{1,0:T(8,128)(2,1)S(1)} %copy-done.3), kind=kOutput, calls=%fused_computation.3 | convolution fusion | flops 471597056 | bytes 5570560 | tf_op jit(solution)/shard_map/rd,rf->df/dot_general | solution.py:445
  101.4 0.1 copy.24
  101.5 0.1 copy.23
  101.7 0.7 pad_maximum_fusion.pw_ref
  102.4 0.1 copy.25
  102.5 0.7 broadcast_select_fusion.pt_ref
  103.2 4.6 %shard_map.111 = (bf16[128,7168]{1,0:T(8,128)(2,1)}, bf16[128,7168]{1,0:T(8,128)(2,1)}) custom-call(bf16[2,4,128,64]{3,2,1,0:T(8,128)(2,1)} %pad_maximum_fusion.pw_ref, bf16[4,128,64]{2,1,0:T(8,128)(2,1)} %broadcast_select_fusion.pt_ref, bf16[4,16,1792]{2,1,0:T(8,128)(2,1)} %get-tuple-element.14.bo_ref, bf16[4,16,1792]{2,1,0:T(8,128)(2,1)} %get-tuple-element.15.bi_ref), custom_call_target="tpu_custom_call" | custom-call | tf_op jit(solution)/shard_map/pallas_call | solution.py:429
  (9 shorter events, 0.1 us)
Async XLA Ops:
  90.7 4.6 %copy-start.1 = (bf16[8,16,7168]{2,1,0:T(8,128)(2,1)S(1)}, bf16[8,16,7168]{2,1,0:T(8,128)(2,1)}, u32[]{:S(2)}) copy-start(bf16[8,16,7168]{2,1,0:T(8,128)(2,1)} %get-tuple-element.22) | copy-start | bytes 5505028
  90.7 4.6 %copy-start.2 = (bf16[128,256]{1,0:T(8,128)(2,1)S(1)}, bf16[128,256]{1,0:T(8,128)(2,1)}, u32[]{:S(2)}) copy-start(bf16[128,256]{1,0:T(8,128)(2,1)} %get-tuple-element.21) | copy-start | bytes 196612
  95.4 3.0 %copy-start = (bf16[8,16,7168]{2,1,0:T(8,128)(2,1)S(1)}, bf16[8,16,7168]{2,1,0:T(8,128)(2,1)}, u32[]{:S(2)}) copy-start(bf16[8,16,7168]{2,1,0:T(8,128)(2,1)} %get-tuple-element.18) | copy-start | bytes 5505028
  95.4 3.0 %copy-start.3 = (bf16[128,256]{1,0:T(8,128)(2,1)S(1)}, bf16[128,256]{1,0:T(8,128)(2,1)}, u32[]{:S(2)}) copy-start(bf16[128,256]{1,0:T(8,128)(2,1)} %get-tuple-element.19) | copy-start | bytes 196612

commit v2 on v1

--- a/solution.py
+++ b/solution.py
@@ -31,10 +31,29 @@
     return jnp.where(hit, 1.0, 0.0).astype(BF16)
 
 
+def routing(route_ref, gates_ref, picked_ref, weight_ref):
+    T = route_ref.shape[0]
+    shape = picked_ref.shape
+    col = lax.broadcasted_iota(jnp.int32, shape, 1)
+    member = jnp.zeros(shape, F32)
+    weight = jnp.zeros(shape, F32)
+    for p in range(route_ref.shape[1]):
+        hit = route_ref[:, p : p + 1] == col // CAP
+        member += jnp.where(hit, 1.0, 0.0)
+        weight += jnp.where(hit, gates_ref[:, p : p + 1], 0.0)
+    row_at = lax.broadcasted_iota(jnp.int32, (T, T), 0)
+    col_at = lax.broadcasted_iota(jnp.int32, (T, T), 1)
+    earlier = jnp.where(col_at < row_at, 1.0, 0.0).astype(BF16)
+    places = mm(earlier, member.astype(BF16))
+    picked = (member > 0.5) & (jnp.abs(places - (col % CAP).astype(F32)) < 0.5)
+    picked_ref[...] = jnp.where(picked, 1.0, 0.0).astype(BF16)
+    weight_ref[...] = jnp.where(picked, weight, 0.0)
+
+
 def exchange(
-    E, L, pq_ref, sg_ref, tok_hbm, cot_hbm, wg_hbm, wu_hbm, wd_hbm,
-    bo_hbm, bi_hbm, xo_hbm, do_hbm, h_ref, a_ref, b_ref,
-    tok, cot, wg, wu, wd, xs, ds, xin, din, xg, dg, gp, up,
+    E, L, route_ref, gates_ref, tok_hbm, cot_hbm, wg_hbm, wu_hbm, wd_hbm,
+    bo_hbm, bi_hbm, xo_hbm, do_hbm, h_ref, a_ref, b_ref, picked_ref, weight_ref,
+    pq, sg, tok, cot, wg, wu, wd, xs, ds, xin, din, xg, dg, gp, up,
     yp, ysib, yline, yret, bo, qp, qsib, qline, qret, bi,
     load_sem, out_sem, disp_s, disp_r, gat_s, gat_r, sib_s, sib_r, line_s, line_r, ret_s, ret_r,
 ):
@@ -75,6 +94,14 @@
         pl.semaphore_signal(barrier, inc=1, device_id=left, device_id_type=MESH)
 
     ends = jnp.where(l > 0, 1, 0) + jnp.where(l < L - 1, 1, 0)
+    routing(route_ref, gates_ref, picked_ref, weight_ref)
+    slot_gate = jnp.sum(weight_ref[...], axis=0, keepdims=True)
+    scale = jnp.zeros((E * ROWS, 1), F32)
+    for q in range(CUTS):
+        at = place((E * ROWS, R), 1, q)
+        pq[q] = mm_nt(at, picked_ref[...]).astype(BF16)
+        scale += jnp.sum(jnp.where(at > 0, slot_gate, 0.0), axis=1, keepdims=True)
+    sg[...] = scale
     pl.semaphore_wait(barrier, E + ends)
 
     def remote(src, dst, ss, rs, dev):
@@ -106,9 +133,9 @@
             at = pl.ds(pl.multiple_of(t * TILE, TILE), TILE)
             acc = jnp.zeros((E * ROWS, TILE), F32)
             for q in range(CUTS):
-                acc += mm(pq_ref[q], src[:, pl.ds(pl.multiple_of(q * W + t * TILE, TILE), TILE)])
+                acc += mm(pq[q], src[:, pl.ds(pl.multiple_of(q * W + t * TILE, TILE), TILE)])
             if scale:
-                acc = acc * sg_ref[...]
+                acc = acc * sg[...]
             dst[:, :, at] = acc.astype(BF16).reshape(E, ROWS, TILE)
             return carry
 
@@ -121,7 +148,8 @@
             part = src[:, :, at].reshape(E * ROWS, TILE)
             for q in range(CUTS):
                 out = mm(place((R, E * ROWS), 0, q), part)
-                dst[blk, :, pl.ds(pl.multiple_of(q * W + t * TILE, TILE), TILE)] = out.astype(BF16)
+                col = pl.ds(pl.multiple_of((q % 2) * W + t * TILE, TILE), TILE)
+                dst[q // 2, blk, :, col] = out.astype(BF16)
             return carry
 
         lax.fori_loop(0, W // TILE, step, 0)
@@ -177,14 +205,14 @@
 
     def total(part, sib, lines, b, j):
         def step(t, carry):
-            at = pl.ds(pl.multiple_of(t * 1024, 1024), 1024)
+            at = pl.ds(pl.multiple_of(t * 512, 512), 512)
             acc = part[b, :, at].astype(F32) + sib[j, :, at].astype(F32)
             for line, k in lines:
                 acc += line[k, :, at].astype(F32)
             part[b, :, at] = acc.astype(BF16)
             return carry
 
-        lax.fori_loop(0, D // 1024, step, 0)
+        lax.fori_loop(0, D // 2 // 512, step, 0)
 
     def r_step(n, part, sib, line, s):
         jl = s - (L - 1 - l)
@@ -213,24 +241,28 @@
         tail(rw, functools.partial(r_copy, n, part, line, jr, 1, right))
 
     def r_last(n, part, sib, line, ret, back):
-        def join(line_slots):
+        def join(h, line_slots):
             def fn():
+                m = 2 * n + h
                 for k in line_slots:
-                    remote(part.at[blk], line.at[k], line_s.at[n, 0], line_r.at[n, k], sibling).wait_recv()
-                total(part, sib, [(line, k) for k in line_slots], blk, l)
+                    remote(
+                        part.at[h].at[blk], line.at[h].at[k], line_s.at[m, 0], line_r.at[m, k], sibling
+                    ).wait_recv()
+                total(part.at[h], sib.at[h], [(line.at[h], k) for k in line_slots], blk, l)
 
             return fn
 
-        pl.when(l == 0)(join([l]))
-        pl.when(l == L - 1)(join([l + 1]))
-        if L > 2:
-            pl.when((l > 0) & (l < L - 1))(join([l, l + 1]))
+        for h in range(2):
+            pl.when(l == 0)(join(h, [l]))
+            pl.when(l == L - 1)(join(h, [l + 1]))
+            if L > 2:
+                pl.when((l > 0) & (l < L - 1))(join(h, [l, l + 1]))
 
         def step(t, carry):
             at = pl.ds(pl.multiple_of(t * TILE, TILE), TILE)
             acc = jnp.zeros((E * ROWS, TILE), F32)
             for q in range(CUTS):
-                own = part[blk, :, pl.ds(pl.multiple_of(q * W + t * TILE, TILE), TILE)]
+                own = part[q // 2, blk, :, pl.ds(pl.multiple_of((q % 2) * W + t * TILE, TILE), TILE)]
                 acc += mm(place((E * ROWS, R), 1, q), own)
             ret[:, :, at] = acc.astype(BF16).reshape(E, ROWS, TILE)
             return carry
@@ -238,6 +270,17 @@
         lax.fori_loop(0, W // TILE, step, 0)
         back[ep] = ret[ep]
         ep_send(n, ret, back, ret_s, ret_r)
+
+    def halves(fn, n, *args):
+        refs = [r for r in args if not isinstance(r, int)]
+        rest = [r for r in args if isinstance(r, int)]
+        for h in range(2):
+            fn(2 * n + h, *[r.at[h] for r in refs], *rest)
+
+    def pass_on(n, buf, s):
+        for h in range(2):
+            g_wait(2 * n + h, buf.at[h], s - 1)
+            g_send(2 * n + h, buf.at[h], s)
 
     loads[0].wait()
     select(tok, xs, xin, False)
@@ -247,22 +290,25 @@
     ep_send(1, ds, din, disp_s, disp_r)
     ep_wait(0, xs, xin, disp_s, disp_r)
     settle(xin, xg)
-    g_send(0, xg, 0)
+    halves(g_send, 0, xg, 0)
     ep_wait(1, ds, din, disp_s, disp_r)
     settle(din, dg)
     for s in range(1, L):
-        g_wait(0, xg, s - 1)
-        g_send(0, xg, s)
-    g_send(1, dg, 0)
-    g_sib(0, xg)
+        pass_on(0, xg, s)
+    halves(g_send, 1, dg, 0)
+    halves(g_sib, 0, xg)
     x_out = pltpu.make_async_copy(xg, xo_hbm, out_sem.at[0])
     x_out.start()
     loads[2].wait()
     loads[3].wait()
 
+    def quarter(buf, t):
+        at = pl.ds(pl.multiple_of((t % 2) * W, TILE), W)
+        return buf[t // 2, :, :, at].reshape(rows, W)
+
     def both(t, carry):
         at = pl.ds(pl.multiple_of(t * W, TILE), W)
-        x = xg[:, :, at].reshape(rows, W)
+        x = quarter(xg, t)
         gp[...] += mm(x, wg[at, :])
         up[...] += mm(x, wu[at, :])
         return carry
@@ -272,59 +318,62 @@
     lax.fori_loop(0, CUTS, both, 0)
     h_ref[...] = (gp[...] * jax.nn.sigmoid(gp[...]) * up[...]).astype(BF16)
     if L > 1:
-        g_wait(1, dg, 0)
-        g_send(1, dg, 1)
+        pass_on(1, dg, 1)
     loads[4].wait()
 
-    def down(t, carry):
-        at = pl.ds(pl.multiple_of(t * 512, 512), 512)
-        yp[:, :, at] = mm(h_ref[...], wd[:, at]).astype(BF16).reshape(2 * L, R, 512)
-        return carry
-
-    lax.fori_loop(0, D // 512, down, 0)
-    s_send(0, yp, ysib)
+    for h in range(2):
+
+        def down(t, carry):
+            at = pl.ds(pl.multiple_of(t * 512, 512), 512)
+            src = pl.ds(pl.multiple_of(h * (D // 2) + t * 512, 512), 512)
+            yp[h, :, :, at] = mm(h_ref[...], wd[:, src]).astype(BF16).reshape(2 * L, R, 512)
+            return carry
+
+        lax.fori_loop(0, D // 2 // 512, down, 0)
+        s_send(h, yp.at[h], ysib.at[h])
     if L > 2:
-        g_wait(1, dg, 1)
-        g_send(1, dg, 2)
-    s_wait(0, yp, ysib)
-    r_step(0, yp, ysib, yline, 0)
+        pass_on(1, dg, 2)
+    for h in range(2):
+        s_wait(h, yp.at[h], ysib.at[h])
+        r_step(h, yp.at[h], ysib.at[h], yline.at[h], 0)
     for s in range(3, L):
-        g_wait(1, dg, s - 1)
-        g_send(1, dg, s)
-        r_step(0, yp, ysib, yline, s - 2)
-    g_sib(1, dg)
+        pass_on(1, dg, s)
+        halves(r_step, 0, yp, ysib, yline, s - 2)
+    halves(g_sib, 1, dg)
     d_out = pltpu.make_async_copy(dg, do_hbm, out_sem.at[1])
     d_out.start()
 
-    hg = jnp.zeros((rows, gp.shape[1]), F32)
-
     def pull(t, carry):
         at = pl.ds(pl.multiple_of(t * W, TILE), W)
-        return carry + mm_nt(dg[:, :, at].reshape(rows, W), wd[:, at])
-
-    hg = lax.fori_loop(0, CUTS, pull, hg)
+        return carry + mm_nt(quarter(dg, t), wd[:, at])
+
+    hg = lax.fori_loop(0, CUTS, pull, jnp.zeros((rows, gp.shape[1]), F32))
     g = gp[...]
     u = up[...]
     sig = jax.nn.sigmoid(g)
     a_ref[...] = (hg * u * (sig * (1.0 + g * (1.0 - sig)))).astype(BF16)
     b_ref[...] = (hg * g * sig).astype(BF16)
+
+    for h in range(2):
+
+        def back_rows(t, carry):
+            at = pl.ds(pl.multiple_of(t * 512, 512), 512)
+            src = pl.ds(pl.multiple_of(h * (D // 2) + t * 512, 512), 512)
+            q = mm_nt(a_ref[...], wg[src, :]) + mm_nt(b_ref[...], wu[src, :])
+            qp[h, :, :, at] = q.astype(BF16).reshape(2 * L, R, 512)
+            return carry
+
+        lax.fori_loop(0, D // 2 // 512, back_rows, 0)
+        s_send(2 + h, qp.at[h], qsib.at[h])
     done = max(1, L - 2)
     if done < L - 1:
-        r_step(0, yp, ysib, yline, done)
-
-    def back_rows(t, carry):
-        at = pl.ds(pl.multiple_of(t * 512, 512), 512)
-        q = mm_nt(a_ref[...], wg[at, :]) + mm_nt(b_ref[...], wu[at, :])
-        qp[:, :, at] = q.astype(BF16).reshape(2 * L, R, 512)
-        return carry
-
-    lax.fori_loop(0, D // 512, back_rows, 0)
-    s_send(1, qp, qsib)
-    s_wait(1, qp, qsib)
-    r_step(1, qp, qsib, qline, 0)
+        halves(r_step, 0, yp, ysib, yline, done)
+    for h in range(2):
+        s_wait(2 + h, qp.at[h], qsib.at[h])
+        r_step(2 + h, qp.at[h], qsib.at[h], qline.at[h], 0)
     r_last(0, yp, ysib, yline, yret, bo)
     for s in range(1, L - 1):
-        r_step(1, qp, qsib, qline, s)
+        halves(r_step, 1, qp, qsib, qline, s)
     ep_wait(0, yret, bo, ret_s, ret_r)
     o_out = pltpu.make_async_copy(bo, bo_hbm, out_sem.at[2])
     o_out.start()
@@ -338,12 +387,27 @@
         cp.wait()
 
 
-def combine(pw_ref, pt_ref, bo_ref, bi_ref, mixed_ref, grad_ref):
+def finish(
+    picked_ref, weight_ref, bo_ref, bi_ref, x_ref, d_ref, h_ref, a_ref, b_ref,
+    mixed_ref, grad_ref, gg_ref, gu_ref, gd_ref,
+):
+    q = pl.program_id(0) // 2
     e_rows = bo_ref.shape[0] * ROWS
     width = bo_ref.shape[2]
+    rows, F = h_ref.shape
+    at = place((picked_ref.shape[1], e_rows), 0, q)
+    weight = weight_ref[...]
+    hi = weight.astype(BF16)
+    lo = (weight - hi.astype(F32)).astype(BF16)
     y = bo_ref[...].reshape(e_rows, width)
-    mixed_ref[...] = (mm(pw_ref[0, 0], y) + mm(pw_ref[1, 0], y)).astype(BF16)
-    grad_ref[...] = mm(pt_ref[0], bi_ref[...].reshape(e_rows, width)).astype(BF16)
+    z = bi_ref[...].reshape(e_rows, width)
+    mixed = mm(mm(hi, at).astype(BF16), y) + mm(mm(lo, at).astype(BF16), y)
+    mixed_ref[...] = mixed.astype(BF16)
+    grad_ref[...] = mm(mm(picked_ref[...], at).astype(BF16), z).astype(BF16)
+    x_t = x_ref[0].reshape(rows, width).T
+    gg_ref[0] = mm(x_t, a_ref[...]).astype(BF16)
+    gu_ref[0] = mm(x_t, b_ref[...]).astype(BF16)
+    gd_ref[0] = mm(h_ref[...].T, d_ref[0].reshape(rows, width)).astype(BF16)
 
 
 def local(tokens, route, gates, cotangent, w_gate, w_up, w_down):
@@ -354,49 +418,32 @@
     R = E * CAP
     rows = 2 * L * R
     F = w_gate.shape[2]
-    matches = route[:, :, None] == jnp.arange(E, dtype=jnp.int32)
-    member = jnp.any(matches, axis=1)
-    weight = jnp.sum(jnp.where(matches, gates[:, :, None], 0.0), axis=1)
-    earlier = jnp.tril(jnp.ones((T, T), BF16), -1)
-    places = mm(earlier, member.astype(BF16)).astype(jnp.int32)
-    picked = member[:, :, None] & (places[:, :, None] == jnp.arange(CAP, dtype=jnp.int32))
-    picked_w = jnp.where(picked, weight[:, :, None], 0.0)
-    slot_gate = jnp.sum(picked_w, axis=0)
-    sg = jnp.broadcast_to(slot_gate[:, None, :], (E, CUTS, CAP)).reshape(E * ROWS, 1)
-    quarter = jnp.eye(CUTS, dtype=bool)[:, None, None, :, None]
-
-    def spread(m):
-        wide = jnp.where(quarter, m[None, :, :, None, :], jnp.zeros((), m.dtype))
-        return wide.reshape(CUTS, T, E * ROWS)
-
-    pt = spread(picked.astype(BF16))
-    pq = pt.transpose(0, 2, 1)
-    hi = picked_w.astype(BF16)
-    lo = (picked_w - hi.astype(F32)).astype(BF16)
-    pw = jnp.stack([spread(hi), spread(lo)])
-
     vm = pl.BlockSpec(memory_space=pltpu.VMEM)
     hbm = pl.BlockSpec(memory_space=pl.ANY)
     sds = jax.ShapeDtypeStruct
     msg = pltpu.VMEM((E, ROWS, W), BF16)
-    allrows = pltpu.VMEM((2 * L, R, D), BF16)
-    own = pltpu.VMEM((L, R, D), BF16)
-    line = pltpu.VMEM((L + 1, R, D), BF16)
+    allrows = pltpu.VMEM((2, 2 * L, R, D // 2), BF16)
+    own = pltpu.VMEM((2, L, R, D // 2), BF16)
+    line = pltpu.VMEM((2, L + 1, R, D // 2), BF16)
     dma = pltpu.SemaphoreType.DMA
-    bo, bi, rows_x, rows_d, hidden, gate_grad, up_grad = pl.pallas_call(
+    bo, bi, rows_x, rows_d, hidden, gate_grad, up_grad, picked, weight = pl.pallas_call(
         functools.partial(exchange, E, L),
         out_shape=(
             sds((E, ROWS, W), BF16),
             sds((E, ROWS, W), BF16),
-            sds((2 * L, R, D), BF16),
-            sds((2 * L, R, D), BF16),
+            sds((2, 2 * L, R, D // 2), BF16),
+            sds((2, 2 * L, R, D // 2), BF16),
             sds((rows, F), BF16),
             sds((rows, F), BF16),
             sds((rows, F), BF16),
+            sds((T, R), BF16),
+            sds((T, R), F32),
         ),
         in_specs=[vm, vm, hbm, hbm, hbm, hbm, hbm],
-        out_specs=(hbm, hbm, hbm, hbm, vm, vm, vm),
+        out_specs=(hbm, hbm, hbm, hbm, vm, vm, vm, vm, vm),
         scratch_shapes=[
+            pltpu.VMEM((CUTS, E * ROWS, T), BF16),
+            pltpu.VMEM((E * ROWS, 1), F32),
             pltpu.VMEM((T, D), BF16),
             pltpu.VMEM((T, D), BF16),
             pltpu.VMEM((D, F), BF16),
@@ -412,39 +459,52 @@
             dma((4,)),
             dma((2, E)),
             dma((2, E)),
-            dma((2, 3, L)),
-            dma((2, 2 * L)),
-            dma((2, L)),
-            dma((2, L)),
-            dma((2, L)),
-            dma((2, L + 1)),
+            dma((4, 3, L)),
+            dma((4, 2 * L)),
+            dma((4, L)),
+            dma((4, L)),
+            dma((4, L)),
+            dma((4, L + 1)),
             dma((2, E)),
             dma((2, E)),
         ],
         compiler_params=pltpu.CompilerParams(
             collective_id=0, has_side_effects=True, vmem_limit_bytes=60 * 1024 * 1024
         ),
-    )(pq, sg, tokens, cotangent, w_gate, w_up, w_down)
-
-    mixed, grad_tokens = pl.pallas_call(
-        combine,
-        grid=(CUTS,),
-        out_shape=(sds((T, D), BF16), sds((T, D), BF16)),
+    )(route, gates, tokens, cotangent, w_gate, w_up, w_down)
+
+    half = W // 2
+    whole = lambda j: (0, 0)
+    return pl.pallas_call(
+        finish,
+        grid=(2 * CUTS,),
+        out_shape=(
+            sds((T, D), BF16),
+            sds((T, D), BF16),
+            sds((1, D, F), BF16),
+            sds((1, D, F), BF16),
+            sds((1, F, D), BF16),
+        ),
         in_specs=[
-            pl.BlockSpec((2, 1, T, E * ROWS), lambda q: (0, q, 0, 0)),
-            pl.BlockSpec((1, T, E * ROWS), lambda q: (q, 0, 0)),
-            pl.BlockSpec((E, ROWS, W), lambda q: (0, 0, 0)),
-            pl.BlockSpec((E, ROWS, W), lambda q: (0, 0, 0)),
+            pl.BlockSpec((T, R), whole),
+            pl.BlockSpec((T, R), whole),
+            pl.BlockSpec((E, ROWS, half), lambda j: (0, 0, j % 2)),
+            pl.BlockSpec((E, ROWS, half), lambda j: (0, 0, j % 2)),
+            pl.BlockSpec((1, 2 * L, R, half), lambda j: (j // 4, 0, 0, j % 4)),
+            pl.BlockSpec((1, 2 * L, R, half), lambda j: (j // 4, 0, 0, j % 4)),
+            pl.BlockSpec((rows, F), whole),
+            pl.BlockSpec((rows, F), whole),
+            pl.BlockSpec((rows, F), whole),
         ],
-        out_specs=(pl.BlockSpec((T, W), lambda q: (0, q)), pl.BlockSpec((T, W), lambda q: (0, q))),
-    )(pw, pt, bo, bi)
-
-    rows_x = rows_x.reshape(rows, D)
-    rows_d = rows_d.reshape(rows, D)
-    grad_down = jnp.einsum("rf,rd->fd", hidden, rows_d, preferred_element_type=F32).astype(BF16)
-    grad_gate = jnp.einsum("rd,rf->df", rows_x, gate_grad, preferred_element_type=F32).astype(BF16)
-    grad_up = jnp.einsum("rd,rf->df", rows_x, up_grad, preferred_element_type=F32).astype(BF16)
-    return (mixed, grad_tokens, grad_gate[None], grad_up[None], grad_down[None])
+        out_specs=(
+            pl.BlockSpec((T, half), lambda j: (0, j)),
+            pl.BlockSpec((T, half), lambda j: (0, j)),
+            pl.BlockSpec((1, half, F), lambda j: (0, j, 0)),
+            pl.BlockSpec((1, half, F), lambda j: (0, j, 0)),
+            pl.BlockSpec((1, F, half), lambda j: (0, 0, j)),
+        ),
+        compiler_params=pltpu.CompilerParams(vmem_limit_bytes=48 * 1024 * 1024),
+    )(picked, weight, bo, bi, rows_x, rows_d, hidden, gate_grad, up_grad)
 
 
 def solution(mesh):

time: 108 us -> 102 us (0.944)
  matrix products: 10.8 us -> 0 us
  local copies, waits for them, and re-layouts: 1.26 us -> 11.8 us
  other arithmetic: 3.77 us -> 0 us
  Pallas kernels: 91.2 us -> 89.3 us
    unnamed x8 -> x20, local copies, waits for them, and re-layouts: 0.02 us -> 11.8 us
    dot_general x4 -> x0, matrix products: 10.8 us -> none  [the longest x1 4.62 us: local(): jnp.einsum('rd,rf->df', rows_x, up_grad, preferred_element_type=F32)]
    pallas_call x1, Pallas kernels: 86.7 us -> 79.8 us  [local(): pl.pallas_call(functools.partial(exchange, E, L), out_shape=(sds((E, ROWS...]
    pallas_call x1, Pallas kernels: 4.57 us -> 9.54 us  [local(): pl.pallas_call(finish, grid=(2 * CUTS,), out_shape=(sds((T, D), BF16), sd...]
    select_n x3 -> x0, other arithmetic: 1.46 us -> none  [spread(): wide = jnp.where(quarter, m[None, :, :, None, :], jnp.zeros((), m.dtype))]
where the time goes in v2:
time: 102 us
  Pallas kernels  89.3 us (88%)
  local copies, waits for them, and re-layouts  11.8 us (12%)
    pallas_call x1, Pallas kernels, local(): pl.pallas_call(functools.partial(exchange, E, L), out_shape=(sds((E, ROWS...  79.8 us
    unnamed x20, local copies, waits for them, and re-layouts  11.8 us
    pallas_call x1, Pallas kernels, local(): pl.pallas_call(finish, grid=(2 * CUTS,), out_shape=(sds((T, D), BF16), sd...  9.54 us

profile of v2, /device:TPU:0, one launch (start us, length us, event | category | flops | bytes accessed | tf_op | source)
XLA Modules:
  0.0 101.8 jit_solution(9801808928876222996)
XLA Ops:
  0.6 1.4 %copy.12.route_ref = s32[128,8]{1,0:T(8,128)} copy(s32[128,8]{0,1:T(8,128)} %param.8) | data formatting | bytes 8192 | tf_op args[1]
  2.0 1.4 %copy.13.gates_ref = f32[128,8]{1,0:T(8,128)} copy(f32[128,8]{0,1:T(8,128)} %param.9) | data formatting | bytes 8192 | tf_op args[2]
  3.5 79.8 %shard_map.110 = (bf16[4,16,1792]{2,1,0:T(8,128)(2,1)}, bf16[4,16,1792]{2,1,0:T(8,128)(2,1)}, bf16[2,8,16,3584]{3,2,1,0:T(8,128)(2,1)}, bf16[2,8,16,3584]{3,2,1,...) custom-call(s32[128,8]{1,0:T(8,128)} %copy.12.route_ref, ...), custom_call_target="tpu_custom_call" | custom-call | tf_op jit(solution)/shard_map/pallas_call | solution.py:429
  83.2 0.0 copy-start
  83.2 1.5 %copy-done = bf16[2,8,16,3584]{3,2,1,0:T(8,128)(2,1)S(1)} copy-done((bf16[2,8,16,3584]{3,2,1,0:T(8,128)(2,1)S(1)}, bf16[2,8,16,3584]{3,2,1,0:T(8,128)(2,1)}, u32[]{:S(2)}) %copy-start) | copy-done | bytes 1835032
  84.7 0.0 copy-start.1
  84.7 1.5 %copy-done.1 = bf16[2,8,16,3584]{3,2,1,0:T(8,128)(2,1)S(1)} copy-done((bf16[2,8,16,3584]{3,2,1,0:T(8,128)(2,1)S(1)}, bf16[2,8,16,3584]{3,2,1,0:T(8,128)(2,1)}, u32[]{:S(2)}) %copy-start.1) | copy-done | bytes 1835032
  86.2 0.0 copy-start.2
  86.2 0.9 copy-done.2
  87.2 0.0 copy-start.3
  87.2 0.9 copy-done.3
  88.1 0.0 copy-start.4
  88.1 0.8 copy-done.4
  88.9 0.0 copy-start.5
  88.9 0.8 copy-done.5
  89.8 0.0 copy-start.6
  89.8 0.8 copy-done.6
  90.6 0.0 copy-start.7
  90.6 0.8 copy-done.7
  91.5 0.0 copy-start.8
  91.5 0.8 copy-done.8
  92.2 9.5 %shard_map.111 = (bf16[128,7168]{1,0:T(8,128)(2,1)}, bf16[128,7168]{1,0:T(8,128)(2,1)}, bf16[1,7168,256]{2,1,0:T(8,128)(2,1)}, bf16[1,7168,256]{2,1,0:T(8,128)(2,1)}, bf16[1,256,7168]{2,1,0:T(8,128)(2,1)}) custom-call(bf16[128,16]{1,0:T(8,128)(2,1)S(1)} %copy-done.8, f32[128,16]{1,0:T(8,128)S(1)} %copy-done.7, bf16[4,16,1792]{2,1,0:T(8,128)(2,1)S(1)} %copy-done.2, ...), custom_call_target="tpu_custom_call" | custom-call | tf_op jit(solution)/shard_map/pallas_call | solution.py:478
Async XLA Ops:
  83.2 1.5 %copy-start = (bf16[2,8,16,3584]{3,2,1,0:T(8,128)(2,1)S(1)}, bf16[2,8,16,3584]{3,2,1,0:T(8,128)(2,1)}, u32[]{:S(2)}) copy-start(bf16[2,8,16,3584]{3,2,1,0:T(8,128)(2,1)} %get-tuple-element.18.x_ref) | copy-start | bytes 5505028
  84.7 1.5 %copy-start.1 = (bf16[2,8,16,3584]{3,2,1,0:T(8,128)(2,1)S(1)}, bf16[2,8,16,3584]{3,2,1,0:T(8,128)(2,1)}, u32[]{:S(2)}) copy-start(bf16[2,8,16,3584]{3,2,1,0:T(8,128)(2,1)} %get-tuple-element.19.d_ref) | copy-start | bytes 5505028
  86.2 0.9 copy-start.2
  87.2 0.9 copy-start.3
  88.1 0.8 copy-start.4
  88.9 0.8 copy-start.5
  89.8 0.8 copy-start.6
  90.6 0.8 copy-start.7
  91.5 0.8 copy-start.8
